TPU v7x, 32 devices: a whole 2x2x4 slice. The times are simulated.
32 devices in a mesh: role: 2 (over y), dp: 16 (over z, x, core).
Axes of the slice: x: 2, y: 2, z: 4, core: 2. Of those that a mesh axis runs over, the one named last changes fastest.
Arguments:
- frames: bfloat16 [2, 128, 121, 2048], P('role', 'dp'), may hold values from -6 to 6
- game_ids: int32 [128], P('dp'), may hold values from 0 to 39, as said below
- taken_actions: int32 [128], P('dp'), may hold values from 0 to 17
- next_actions: int32 [128], P('dp'), may hold values from 0 to 17
- expert_flags: int32 [128], P('dp'), may hold values 0 or 1
- rewards: float32 [128], P('dp'), may hold values from -1 to 1
- done_flags: int32 [128], P('dp'), may hold values 0 or 1
- weight_in: float32 [1, 2048, 512], P(None, 'dp'), may hold values from -0.125 to 0.125
- weight_mid: float32 [1, 4608, 512], P(None, 'dp'), may hold values from -0.09375 to 0.09375
- weight_out: float32 [1, 512, 2048], P(None, 'dp'), may hold values from -0.25 to 0.25
- norm_gains: float32 [1, 6144], P(None, 'dp'), may hold values from 0.5 to 1.5
- head_table: float32 [2048, 36720], P('dp'), may hold values from -0.125 to 0.125
- moment_in: float32 [1, 2048, 512], P(None, 'dp'), may hold values from -0.046875 to 0.046875
- moment_mid: float32 [1, 4608, 512], P(None, 'dp'), may hold values from -0.046875 to 0.046875
- moment_out: float32 [1, 512, 2048], P(None, 'dp'), may hold values from -0.046875 to 0.046875
- moment_gains: float32 [1, 6144], P(None, 'dp'), may hold values from -0.15625 to 0.15625
- moment_head: float32 [2048, 36720], P('dp'), may hold values from -0.046875 to 0.046875
- average_in: float32 [1, 2048, 512], P(None, 'dp'), may hold values from -0.125 to 0.125
- average_mid: float32 [1, 4608, 512], P(None, 'dp'), may hold values from -0.09375 to 0.09375
- average_out: float32 [1, 512, 2048], P(None, 'dp'), may hold values from -0.25 to 0.25
- average_gains: float32 [1, 6144], P(None, 'dp'), may hold values from 0.5 to 1.5
- average_head: float32 [2048, 36720], P('dp'), may hold values from -0.125 to 0.125
Outputs:
- loss_total: float32 [], replicated
- new_weight_in: float32 [1, 2048, 512], P(None, 'dp', 'role')
- gradient_in: float32 [1, 2048, 512], P(None, 'dp', 'role')
- new_average_in: float32 [1, 2048, 512], P(None, 'dp', 'role')
- copy_weight_in: bfloat16 [1, 2048, 512], P(None, 'dp', 'role')
- new_weight_mid: float32 [1, 4608, 512], P(None, 'dp', 'role')
- new_moment_mid: float32 [1, 4608, 512], P(None, 'dp', 'role')
- new_average_mid: float32 [1, 4608, 512], P(None, 'dp', 'role')
- copy_weight_mid: bfloat16 [1, 4608, 512], P(None, 'dp', 'role')
- new_weight_out: float32 [1, 512, 2048], P(None, 'dp', 'role')
- new_moment_out: float32 [1, 512, 2048], P(None, 'dp', 'role')
- new_average_out: float32 [1, 512, 2048], P(None, 'dp', 'role')
- copy_weight_out: bfloat16 [1, 512, 2048], P(None, 'dp', 'role')
- new_norm_gains: float32 [1, 6144], P(None, 'dp')
- new_moment_gains: float32 [1, 6144], P(None, 'dp')
- new_average_gains: float32 [1, 6144], P(None, 'dp')
- copy_norm_gains: bfloat16 [1, 6144], P(None, 'dp')
- new_head_table: float32 [2048, 36720], P('dp', 'role')
- new_moment_head: float32 [2048, 36720], P('dp', 'role')
- new_average_head: float32 [2048, 36720], P('dp', 'role')
- copy_head_table: bfloat16 [2048, 36720], P('dp', 'role')
Inputs may be any that keep to these rules, and one draw needn't show every extreme that they name: `game_ids`: 10 of the games, never game 0 nor game 40 - 1, are never drawn; which ones is drawn from the seed; the other games are equally likely.
All inputs are finite; a program needn't handle non-finite values. No bound on the sum of `expert_flags` or of `done_flags` on one device may be relied on, other than what follows from the above.
Results may differ from a plain program's by a relative error of at most 0.015.
Values may be sent and summed in bfloat16 or wider, within the bound.
A program may use at most 320 MiB of HBM per device.

v0:
```python
import functools

import jax
import jax.numpy as jnp
import numpy as np
from jax import lax
from jax.experimental import pallas as pl
from jax.experimental.pallas import tpu as pltpu
from jax.sharding import PartitionSpec as P

D = 2048
MID = 512
GAMES = 40
ACTIONS = 18
ATOMS = 51
GROUPS = 32
SIDE = 11
LAYERS = 1


support_low = -10.0
support_high = 10.0
discount = 0.99
penalty = 0.05
momentum_decay = 0.5
average_decay = 0.5
learn_rate = 4.0
gain_rate = 40.0
epsilon = 1e-05
HIGHEST = lax.Precision.HIGHEST


def passed_along(block, axis, distance):
    devices = range(lax.axis_size(axis))
    route = [(i - distance, i) for i in devices if i - distance in devices]
    return lax.ppermute(block, axis, route)


def split_gains(gains):
    return (
        gains[:MID],
        gains[MID : 2 * MID],
        gains[2 * MID : 3 * MID],
        gains[3 * MID : 4 * MID],
        gains[4 * MID : 4 * MID + D],
        gains[4 * MID + D :],
    )


def group_norm(values, gain, shift):
    rows, pixels, width = values.shape
    grouped = values.reshape(rows, pixels, GROUPS, width // GROUPS)
    center = grouped - jnp.mean(grouped, axis=(1, 3), keepdims=True)
    spread = jnp.mean(center * center, axis=(1, 3), keepdims=True)
    normed = (center * lax.rsqrt(spread + epsilon)).reshape(values.shape)
    return normed * gain + shift


def patches_of(acts):
    rows, pixels, width = acts.shape
    grid = acts.reshape(rows, SIDE, SIDE, width)
    padded = jnp.pad(grid, ((0, 0), (1, 1), (1, 1), (0, 0)))
    pieces = [
        padded[:, down : down + SIDE, right : right + SIDE, :]
        for down in range(3)
        for right in range(3)
    ]
    return jnp.concatenate(pieces, axis=-1).reshape(rows, pixels, 9 * width)


def transition_loss(logits, target_dist, action_hot, expert, support):
    log_prob = jax.nn.log_softmax(logits, axis=-1)
    values = jnp.sum(jnp.exp(log_prob) * support, axis=-1)
    spread_sum = jax.nn.logsumexp(values, axis=-1)
    chosen_log = jnp.sum(log_prob * action_hot[:, :, None], axis=1)
    cross = -jnp.sum(target_dist * chosen_log, axis=-1)
    regular = spread_sum - jnp.sum(values * action_hot, axis=-1)
    return cross + penalty * expert * regular


def project_target(next_prob, rewards, done_f, support):
    moved = jnp.clip(
        rewards[:, None] + discount * (1.0 - done_f)[:, None] * support[None, :],
        support_low,
        support_high,
    )
    spacing = (support_high - support_low) / (ATOMS - 1)
    weight = jnp.maximum(0.0, 1.0 - jnp.abs(moved[:, :, None] - support[None, None, :]) / spacing)
    return jnp.sum(next_prob[:, :, None] * weight, axis=1)


def renew(weight, grad, moment, average, rate):
    new_moment = momentum_decay * moment + grad
    new_weight = weight - rate * (grad + momentum_decay * new_moment)
    new_average = average_decay * average + (1.0 - average_decay) * new_weight
    return (new_weight, new_moment, new_average, new_weight.astype(jnp.bfloat16))


def lower_half(values):
    return values[..., : values.shape[-1] // 2]


def upper_half(values):
    return values[..., values.shape[-1] // 2 :]


def own_half(values, role_index):
    half = values.shape[-1] // 2
    return lax.dynamic_slice_in_dim(values, role_index * half, half, values.ndim - 1)


def norm_act(hidden, gain, shift):
    return jax.nn.gelu(group_norm(hidden, gain, shift))


def outer_act(hidden, gain, shift, stream):
    return jax.nn.gelu(stream + group_norm(hidden, gain, shift))


def block_forward(stream, weights):
    w_in, w_mid, w_out, gains = weights
    gain_one, shift_one, gain_two, shift_two, gain_three, shift_three = split_gains(gains)
    stream_low = stream.astype(jnp.bfloat16)
    hidden_in = jnp.einsum("bpc,cm->bpm", stream_low, w_in, preferred_element_type=jnp.float32)
    act_in = norm_act(hidden_in, gain_one, shift_one).astype(jnp.bfloat16)
    hidden_mid = jnp.einsum(
        "bpc,cm->bpm", patches_of(act_in), w_mid, preferred_element_type=jnp.float32
    )
    act_mid = norm_act(hidden_mid, gain_two, shift_two).astype(jnp.bfloat16)
    hidden_out = jnp.einsum("bpc,cm->bpm", act_mid, w_out, preferred_element_type=jnp.float32)
    result = outer_act(hidden_out, gain_three, shift_three, stream)
    return (result, (stream, stream_low, hidden_in, act_in, hidden_mid, act_mid, hidden_out))


def block_backward(grad_result, weights, kept, settle):
    w_in, w_mid, w_out, gains = weights
    stream, stream_low, hidden_in, act_in, hidden_mid, act_mid, hidden_out = kept
    gain_one, shift_one, gain_two, shift_two, gain_three, shift_three = split_gains(gains)
    _, back_three = jax.vjp(outer_act, hidden_out, gain_three, shift_three, stream)
    d_three, dg_three, db_three, d_resid = back_three(grad_result)
    d_three = d_three.astype(jnp.bfloat16)
    grad_out = settle(
        jnp.einsum("bpm,bpc->mc", act_mid, d_three, preferred_element_type=jnp.float32)
    )
    d_act_mid = jnp.einsum("bpc,mc->bpm", d_three, w_out, preferred_element_type=jnp.float32)
    _, back_two = jax.vjp(norm_act, hidden_mid, gain_two, shift_two)
    d_two, dg_two, db_two = back_two(d_act_mid)
    d_two = d_two.astype(jnp.bfloat16)
    grad_mid = settle(
        jnp.einsum("bpk,bpm->km", patches_of(act_in), d_two, preferred_element_type=jnp.float32)
    )
    d_cols = jnp.einsum("bpm,km->bpk", d_two, w_mid, preferred_element_type=jnp.float32)
    _, back_cols = jax.vjp(patches_of, act_in.astype(jnp.float32))
    (d_act_in,) = back_cols(d_cols)
    _, back_one = jax.vjp(norm_act, hidden_in, gain_one, shift_one)
    d_one, dg_one, db_one = back_one(d_act_in)
    d_one = d_one.astype(jnp.bfloat16)
    grad_in = jnp.einsum("bpc,bpm->cm", stream_low, d_one, preferred_element_type=jnp.float32)
    d_stream = d_resid + jnp.einsum("bpm,cm->bpc", d_one, w_in, preferred_element_type=jnp.float32)
    grad_gains = jnp.concatenate([dg_one, db_one, dg_two, db_two, dg_three, db_three])
    grad_in, grad_gains = settle((grad_in, grad_gains))
    return (d_stream, (grad_in, grad_mid, grad_out, grad_gains))


def on_device(
    frames,
    game_ids,
    taken_actions,
    next_actions,
    expert_flags,
    rewards,
    done_flags,
    weight_in,
    weight_mid,
    weight_out,
    norm_gains,
    head_table,
    moment_in,
    moment_mid,
    moment_out,
    moment_gains,
    moment_head,
    average_in,
    average_mid,
    average_out,
    average_gains,
    average_head,
):
    role_index = lax.axis_index("role")
    online = role_index == 0
    use_in = jnp.where(online, weight_in, average_in).astype(jnp.bfloat16)
    use_mid = jnp.where(online, weight_mid, average_mid).astype(jnp.bfloat16)
    use_out = jnp.where(online, weight_out, average_out).astype(jnp.bfloat16)
    use_gains = jnp.where(online, norm_gains, average_gains).astype(jnp.bfloat16)
    use_head = jnp.where(online, head_table, average_head).astype(jnp.bfloat16)
    support = support_low + (support_high - support_low) * jnp.arange(ATOMS, dtype=jnp.float32) / (
        ATOMS - 1
    )
    own_hot = (game_ids[:, None] == lax.broadcasted_iota(jnp.int32, (1, GAMES), 1)).astype(
        jnp.float32
    )
    counts = jnp.sum(own_hot, axis=0)
    stream = frames[0].astype(jnp.float32)
    layer = 0
    pieces = (
        lax.all_gather(use_in[layer], "dp", axis=0, tiled=True),
        lax.all_gather(use_mid[layer], "dp", axis=0, tiled=True),
        lax.all_gather(use_out[layer], "dp", axis=0, tiled=True),
        lax.all_gather(use_gains[layer], "dp", axis=0, tiled=True),
    )
    weights = (pieces[0], pieces[1], pieces[2], pieces[3].astype(jnp.float32))
    stream, saved = block_forward(stream, weights)
    gathered = [weights]
    kept = [saved]
    trans = stream.shape[0]
    pixels = stream.shape[1]
    wide_k = ACTIONS * ATOMS
    head_rows = head_table.shape[0]
    feat_low = jnp.mean(stream, axis=1).astype(jnp.bfloat16)
    feat_all, game_all = (
        lax.all_gather(feat_low, "dp", axis=0, tiled=True),
        lax.all_gather(game_ids.astype(jnp.bfloat16)[:, None], "dp", axis=0, tiled=True),
    )
    game_iota = lax.broadcasted_iota(jnp.int32, (1, GAMES), 1).astype(jnp.float32)
    all_hot = (game_all.astype(jnp.float32) == game_iota).astype(jnp.bfloat16)
    feat_rows = lax.dynamic_slice_in_dim(feat_all, lax.axis_index("dp") * head_rows, head_rows, 1)
    head_low = use_head.reshape(head_rows * GAMES, wide_k)

    def widen(count):
        spread_rows = (feat_rows[:, :, None] * all_hot[:, None, :]).reshape(
            count, head_rows * GAMES
        )
        return (spread_rows, all_hot)

    spread_rows, hot_piece = widen(trans * lax.axis_size("dp"))
    flat_logits = lax.psum_scatter(
        jnp.dot(spread_rows, head_low, preferred_element_type=jnp.float32),
        "dp",
        scatter_dimension=0,
        tiled=True,
    )
    logits = flat_logits.reshape(trans, ACTIONS, ATOMS)
    next_hot = (next_actions[:, None] == lax.broadcasted_iota(jnp.int32, (1, ACTIONS), 1)).astype(
        jnp.float32
    )
    next_prob = jax.nn.softmax(jnp.sum(logits * next_hot[:, :, None], axis=1), axis=-1)
    projected = project_target(next_prob, rewards, done_flags.astype(jnp.float32), support)
    target_dist = passed_along(projected, "role", -1)
    action_hot = (
        taken_actions[:, None] == lax.broadcasted_iota(jnp.int32, (1, ACTIONS), 1)
    ).astype(jnp.float32)
    expert = expert_flags.astype(jnp.float32)

    def local_loss(values):
        return transition_loss(values, target_dist, action_hot, expert, support)

    row_loss, loss_back = jax.vjp(local_loss, logits)
    sums = jnp.dot(row_loss, own_hot, precision=HIGHEST)
    total_counts, total_sums = lax.psum((counts, sums), "dp")
    floor_counts = jnp.maximum(total_counts, 1.0)
    loss_total = jnp.sum(total_sums / floor_counts)
    row_weight = jnp.dot(own_hot, 1.0 / (GAMES * floor_counts), precision=HIGHEST)
    (d_logits,) = loss_back(row_weight)
    d_low = d_logits.reshape(trans, wide_k).astype(jnp.bfloat16)
    piece = lax.all_gather(d_low, "dp", axis=0, tiled=True)
    count = piece.shape[0]
    spread_rows, hot_piece = widen(count)
    grad_head = lax.dot_general(
        spread_rows, piece, (((0,), (0,)), ((), ())), preferred_element_type=jnp.float32
    )
    back_wide = jnp.dot(piece, head_low.T, preferred_element_type=jnp.float32)
    back_rows = jnp.sum(
        back_wide.reshape(count, head_rows, GAMES) * hot_piece[:, None, :].astype(jnp.float32),
        axis=2,
    )
    grad_rows = back_rows
    grad_head, grad_rows = (grad_head, grad_rows)
    feat_grad = lax.all_to_all(
        grad_rows.astype(jnp.bfloat16), "dp", split_axis=0, concat_axis=1, tiled=True
    ).astype(grad_rows.dtype)
    d_stream = jnp.broadcast_to(feat_grad[:, None, :] / pixels, stream.shape)

    def settle(values):
        return values

    layer_grads = [None] * LAYERS
    for layer in reversed(range(LAYERS)):
        d_stream, block_grad = block_backward(d_stream, gathered[layer], kept[layer], settle)
        layer_grads[layer] = block_grad
    stacked = tuple((jnp.stack([layer_grads[0][kind]]) for kind in range(4)))
    reduced = lax.psum_scatter(stacked, "dp", scatter_dimension=1, tiled=True)
    head_grad = grad_head.reshape(head_rows, GAMES * wide_k)
    sent = (
        passed_along(upper_half(reduced[0]).astype(jnp.bfloat16), "role", 1).astype(jnp.float32),
        passed_along(upper_half(reduced[1]).astype(jnp.bfloat16), "role", 1).astype(jnp.float32),
        passed_along(upper_half(reduced[2]).astype(jnp.bfloat16), "role", 1).astype(jnp.float32),
        passed_along(reduced[3].astype(jnp.bfloat16), "role", 1).astype(jnp.float32),
        passed_along(upper_half(head_grad).astype(jnp.bfloat16), "role", 1).astype(jnp.float32),
        passed_along(loss_total.astype(jnp.bfloat16), "role", 1).astype(loss_total.dtype),
    )
    grad_in = jnp.where(online, lower_half(reduced[0]), sent[0])
    grad_mid = jnp.where(online, lower_half(reduced[1]), sent[1])
    grad_out = jnp.where(online, lower_half(reduced[2]), sent[2])
    grad_gains = jnp.where(online, reduced[3], sent[3])
    grad_table = jnp.where(online, lower_half(head_grad), sent[4])
    loss_out = jnp.where(online, loss_total, sent[5])
    in_w, in_m, in_a, in_c = renew(
        own_half(weight_in, role_index),
        grad_in,
        own_half(moment_in, role_index),
        own_half(average_in, role_index),
        learn_rate,
    )
    mid_w, mid_m, mid_a, mid_c = renew(
        own_half(weight_mid, role_index),
        grad_mid,
        own_half(moment_mid, role_index),
        own_half(average_mid, role_index),
        learn_rate,
    )
    out_w, out_m, out_a, out_c = renew(
        own_half(weight_out, role_index),
        grad_out,
        own_half(moment_out, role_index),
        own_half(average_out, role_index),
        learn_rate,
    )
    gain_w, gain_m, gain_a, gain_c = renew(
        norm_gains, grad_gains, moment_gains, average_gains, gain_rate
    )
    head_w, head_m, head_a, head_c = renew(
        own_half(head_table, role_index),
        grad_table,
        own_half(moment_head, role_index),
        own_half(average_head, role_index),
        learn_rate,
    )
    return (
        loss_out,
        in_w,
        grad_in,
        in_a,
        in_c,
        mid_w,
        mid_m,
        mid_a,
        mid_c,
        out_w,
        out_m,
        out_a,
        out_c,
        gain_w,
        gain_m,
        gain_a,
        gain_c,
        head_w,
        head_m,
        head_a,
        head_c,
    )


MESH = pl.DeviceIdType.MESH


def any_spec():
    return pl.BlockSpec(memory_space=pl.ANY)


def greet(peers):
    barrier = pltpu.get_barrier_semaphore()
    for cond, dev in peers:
        def go(dev=dev):
            pl.semaphore_signal(barrier, inc=1, device_id=dev, device_id_type=MESH)
        go() if cond is None else pl.when(cond)(go)
    count = sum(1 for cond, _ in peers if cond is None)
    for cond, _ in peers:
        if cond is not None:
            count = count + cond.astype(jnp.int32)
    pl.semaphore_wait(barrier, count)


def place():
    me = lax.axis_index("dp")
    core = lax.rem(me, 2)
    x = lax.rem(me // 2, 2)
    z = me // 4
    return me, z, x, core


D = 2048
MID = 512
GROUPS = 32
SIDE = 11
PIX = 121
TB = 8
PITCH = 12
RB = PITCH * TB
VR = SIDE * TB
ROWS = SIDE * RB
PAD = 16 * TB
EROWS = 164 * TB
BLK = 352
CH = 512
epsilon = 1e-05
GK = 0.7978845608028654
GC = 0.044715
OFFS = [(i - 1) * PITCH + (j - 1) for i in range(3) for j in range(3)]


def group_sum(v, gs):
    width = v.shape[1]
    n = width // 128
    a = lax.broadcasted_iota(jnp.int32, (128, 128), 0) // gs
    b = lax.broadcasted_iota(jnp.int32, (128, 128), 1) // gs
    m = (a == b).astype(jnp.float32)
    st = jnp.concatenate([v[:, k * 128:(k + 1) * 128] for k in range(n)], axis=0)
    r = jnp.dot(st, m, precision=lax.Precision.HIGHEST, preferred_element_type=jnp.float32)
    return jnp.concatenate([r[k * 8:(k + 1) * 8] for k in range(n)], axis=1)


def fold(v):
    rows, w = v.shape
    return jnp.sum(v.reshape(rows // TB, TB, w), axis=0)


def moments(h_ref, lo, gs):
    def one(r, acc):
        return acc + fold(h_ref[pl.ds(pl.multiple_of(r * RB, RB), VR), lo:lo + CH])
    s = lax.fori_loop(0, SIDE, one, jnp.zeros((TB, CH), jnp.float32))
    mean = group_sum(s, gs) / float(PIX * gs)

    def two(r, acc):
        h = h_ref[pl.ds(pl.multiple_of(r * RB, RB), VR), lo:lo + CH].reshape(SIDE, TB, CH) - mean[None]
        return acc + jnp.sum(h * h, axis=0)
    q = lax.fori_loop(0, SIDE, two, jnp.zeros((TB, CH), jnp.float32))
    var = group_sum(q, gs) / float(PIX * gs)
    return mean, lax.rsqrt(var + epsilon)


def gelu(u):
    return 0.5 * u * (1.0 + jnp.tanh(GK * (u + GC * (u * u * u))))


def dgelu(u):
    uu = u * u
    t = jnp.tanh(GK * u * (1.0 + GC * uu))
    return 0.5 * (1.0 + t) + 0.5 * u * (1.0 - t * t) * (GK + (3.0 * GK * GC) * uu)


def shifted(e_ref, o_ref, s, row, n):
    ref, base = (e_ref, 16 + s) if s % 2 == 0 else (o_ref, 17 + s)
    return ref[pl.ds(pl.multiple_of(row + base * TB, 16), n), :]


def put_shifted(e_ref, o_ref, r, v):
    z = jnp.zeros((TB, v.shape[1]), jnp.float32)
    at = pl.ds(pl.multiple_of(PAD + r * RB, 16), RB)
    e_ref[at, :] = jnp.concatenate([v, z], axis=0).astype(jnp.bfloat16)
    o_ref[at, :] = jnp.concatenate([z, v], axis=0).astype(jnp.bfloat16)


def clear_margins(e_ref, o_ref):
    z = jnp.zeros((PAD, MID), jnp.bfloat16)
    for ref in (e_ref, o_ref):
        ref[0:PAD, :] = z
        ref[PAD + ROWS:EROWS, :] = z


def row_at(r):
    return pl.ds(pl.multiple_of(r * RB, RB), VR)


def rows_full(r):
    return pl.ds(pl.multiple_of(r * RB, RB), RB)


def norm_back(h_ref, lo, dy_ref, mean, rstd, gain, gs, s1, s2, emit):
    n = 1.0 / float(PIX * gs)
    m1 = group_sum(gain * s1, gs) * n
    m2 = group_sum(gain * s2, gs) * n
    ca = rstd * gain
    cc = -rstd * rstd * m2
    cb = -rstd * m1 - mean * cc

    def one(r, c):
        h = h_ref[row_at(r), lo:lo + CH].reshape(SIDE, TB, CH)
        dy = dy_ref[row_at(r), :].reshape(SIDE, TB, CH)
        emit(r, (ca[None] * dy + cc[None] * h + cb[None]).reshape(VR, CH))
        return c
    lax.fori_loop(0, SIDE, one, 0)


D = 2048
GAMES = 40
ACTIONS = 18
ATOMS = 51
WIDE = ACTIONS * ATOMS
LW = 1024
WIN = 1024
COLS = GAMES * WIDE
HALF = COLS // 2
PADC = 36864
TB = 8
support_low = -10.0
support_high = 10.0
discount = 0.99
penalty = 0.05


def window_of(g):
    return (WIDE * g) // 16 * 16


def ids_offset(ids):
    return lax.bitwise_and(WIDE * ids, 15)


def shift_rows(v, off, right):
    width = v.shape[1]
    for b in range(1, 4):
        n = 1 << b
        bit = lax.bitwise_and(off, n) != 0
        bit = jnp.concatenate([bit.astype(jnp.float32)] * (width // 128), axis=1) > 0.5
        v = jnp.where(bit, pltpu.roll(v, n if right else width - n, 1), v)
    return v


def widen(dl):
    n = dl.shape[0]
    v = dl.astype(jnp.float32)
    v = jnp.concatenate([v[:, 0:TB], v[:, TB:2 * TB]], axis=2).reshape(n * TB, LW)
    lanes = lax.broadcasted_iota(jnp.int32, (n * TB, 128), 1)
    last = jnp.where(lanes < WIDE - LW + 128, v[:, LW - 128:], 0.0)
    return jnp.concatenate([v[:, :LW - 128], last], axis=1)


W_IN, W_MID, W_OUT, MISC = 0, 1, 2, 3
HC = 2048
NHC = -(-COLS // HC)
T0 = (((0,), (0,)), ((), ()))
T1 = (((1,), (1,)), ((), ()))


def rc(src, dst, ss, rs, dev):
    return pltpu.make_async_remote_copy(src_ref=src, dst_ref=dst, send_sem=ss, recv_sem=rs, device_id=dev,
                                        device_id_type=MESH)


def when(cond, do):
    if cond is None:
        do()
    else:
        pl.when(cond)(do)


class Gather:
    def __init__(self, nz, own, full, rows, own_sem, send, recv):
        self.nz, self.own_refs, self.full, self.rows = nz, own, full, rows
        self.own_sem, self.send, self.recv = own_sem, send, recv
        self.me, self.z, self.x, self.c = place()
        me, x, c = self.me, self.x, self.c
        self.up, self.down = {"dp": me + 4}, {"dp": me - 4}
        self.xp, self.cp = {"dp": me + 2 - 4 * x}, {"dp": me + 1 - 2 * c}
        self.has_up, self.has_down = self.z < nz - 1, self.z > 0
        self.started = []

    def slot(self, a, i):
        n = self.rows[a]
        return self.full[a].at[i] if n is None else self.full[a].at[pl.ds(pl.multiple_of(i * n, 16), n)]

    def put(self, cond, a, src, i, dev, k):
        d = rc(src, self.slot(a, i), self.send.at[a, k], self.recv.at[a, i], dev)
        when(cond, d.start)
        self.started.append((cond, d))

    def take(self, cond, a, i):
        d = rc(self.slot(a, i), self.slot(a, i), self.send.at[a, 0], self.recv.at[a, i], self.cp)
        when(cond, d.wait_recv)

    def begin(self, a):
        src = self.own_refs[a]
        self.put(self.has_up, a, src, self.me, self.up, 0)
        self.put(self.has_down, a, src, self.me, self.down, 1)
        self.put(None, a, src, self.me, self.xp, 2)
        self.put(None, a, src, self.me, self.cp, 3)
        pltpu.make_async_copy(src, self.slot(a, self.me), self.own_sem.at[a]).start()

    def along_z(self, a, d):
        k = 4 + (d - 1) * 6
        for up in (True, False):
            s = self.me - 4 * d if up else self.me + 4 * d
            ok = self.z - d >= 0 if up else self.z + d < self.nz
            more = jnp.logical_and(ok, self.has_up if up else self.has_down)
            m = k if up else k + 3
            self.take(ok, a, s)
            self.put(more, a, self.slot(a, s), s, self.up if up else self.down, m)
            self.put(ok, a, self.slot(a, s), s, self.xp, m + 1)
            self.put(ok, a, self.slot(a, s), s, self.cp, m + 2)

    def at_distance(self, d):
        for up in ((True,) if d == 0 else (False, True)):
            zz = self.z + d if up else self.z - d
            yield zz, (None if d == 0 else zz < self.nz if up else zz >= 0), up

    def along_x(self, a, d):
        k = 4 + (self.nz - 1) * 6
        for zz, ok, up in self.at_distance(d):
            s = zz * 4 + (1 - self.x) * 2 + self.c
            self.take(ok, a, s)
            self.put(ok, a, self.slot(a, s), s, self.cp, k + 2 * d + (1 if up else 0))

    def arrived(self, a):
        for d in range(self.nz):
            for zz, ok, _ in self.at_distance(d):
                for xx in (self.x, 1 - self.x):
                    self.take(ok, a, zz * 4 + xx * 2 + 1 - self.c)
        pltpu.make_async_copy(self.own_refs[a], self.slot(a, self.me), self.own_sem.at[a]).wait()

    def end(self):
        for cond, d in self.started:
            when(cond, d.wait_send)


def put_gain(gg_ref, at, s):
    gg_ref[:, at:at + CH] = jnp.sum(s, axis=0, keepdims=True)


def through(h_ref, d2_ref, st_ref, g_ref, gg_ref, at, goff, boff, emit):
    z8 = jnp.zeros((TB, CH), jnp.float32)
    mean = st_ref[0:8, at:at + MID]
    rstd = st_ref[8:16, at:at + MID]
    gain = g_ref[:, goff:goff + MID]
    shift = g_ref[:, boff:boff + MID]
    mr = mean * rstd

    def one(r, acc):
        s1, s2 = acc
        h = h_ref[row_at(r), :].reshape(SIDE, TB, MID)
        da = d2_ref[row_at(r), :].reshape(SIDE, TB, MID)
        xh = h * rstd[None] - mr[None]
        dy = da * dgelu(xh * gain + shift)
        d2_ref[row_at(r), :] = dy.reshape(VR, MID)
        return s1 + jnp.sum(dy, axis=0), s2 + jnp.sum(dy * xh, axis=0)
    s1, s2 = lax.fori_loop(0, SIDE, one, (z8, z8))
    put_gain(gg_ref, goff, s2)
    put_gain(gg_ref, boff, s1)
    norm_back(h_ref, 0, d2_ref, mean, rstd, gain, MID // GROUPS, s1, s2, emit)


def step_kernel(n, fr_hbm, wi, wm, wo, wg, ai, am, ao, ag, k0, k1, k2, k3, k4, k5, ht_hbm, ha_hbm,
                x_hbm, h1_hbm, a2_hbm, dh3_hbm, e_hbm, o_hbm, wmid_hbm, fart_hbm,
                st_ref, g_ref, gg_ref, gall_ref, frow_ref, dlog_ref, loss_ref,
                scal_ref, own_in, own_mid, own_out, own_misc, win_ref, wmid_ref, wout_ref, misc_ref,
                x_ref, h1_ref, h2_ref, h3_ref, a2_ref, dfeat_ref, sl_ref, e_ref, o_ref,
                d2_ref, dh3_ref, far_ref, fart_ref, fbuf, hbuf, head_ref,
                fsend, frecv, part, r1, r2, tgt_s, tgt_r, down_s, dsend, drecv,
                own_sem, g_send, g_recv, f_sem, h_sem, k_sem, ss, rs_,
                s_f, q_f, s_1, q_1, s_2, q_2, s_t, q_t, s_l, q_l, s_c, q_c, s_d, q_d, s_r, q_r):
    me, z, x, c = place()
    role = lax.axis_index("role")
    half = n // 2
    peers = [lax.rem(me + k, n) for k in range(1, n)]
    cp = me + 1 - 2 * c
    du_ref = d2_ref

    def pick(w, a, dst):
        def fill(src):
            dst[...] = src[...].astype(jnp.bfloat16)
        pl.when(role == 0)(lambda: fill(w))
        pl.when(role != 0)(lambda: fill(a))

    def fetch_frames(r):
        return pltpu.make_async_copy(fr_hbm.at[pl.ds(r * SIDE, SIDE)], fbuf.at[r % 2], f_sem.at[r % 2])

    def fetch_head(k, go):
        m = HC if k < NHC - 1 else COLS - (NHC - 1) * HC

        def one(src):
            d = pltpu.make_async_copy(src.at[pl.ds(k * HC, m)], hbuf.at[k % 2, pl.ds(0, m)], h_sem.at[k % 2])
            d.start() if go else d.wait()
        if go:
            pl.when(role == 0)(lambda: one(ht_hbm))
            pl.when(role != 0)(lambda: one(ha_hbm))
        else:
            one(ht_hbm)
    fetch_frames(0).start()
    fetch_head(0, True)
    pick(wi, ai, own_in)
    pick(wm, am, own_mid)
    pick(wo, ao, own_out)

    def pick_gains(src):
        v = src[...].astype(jnp.bfloat16).astype(jnp.float32)
        for k in range(3):
            own_misc[k:k + 1, :] = v[:, k * 128:(k + 1) * 128]
    own_misc[0:TB, :] = jnp.zeros((TB, 128), jnp.float32)
    pl.when(role == 0)(lambda: pick_gains(wg))
    pl.when(role != 0)(lambda: pick_gains(ag))
    for k, ref in enumerate((k0, k1, k2, k3, k4, k5)):
        for t in range(TB):
            scal_ref[k, t:t + 1, :] = jnp.full((1, 128), ref[t].astype(jnp.float32), jnp.float32)
    own_misc[TB:2 * TB, :] = scal_ref[5]
    greet([(None, {"dp": p}) for p in peers] + [(None, {"role": 1 - role})])

    gath = Gather(n // 4, (own_in, own_mid, own_out, own_misc), (win_ref, wmid_ref, wout_ref, misc_ref),
               (D // n, 9 * MID // n, MID // n, None), own_sem, g_send, g_recv)
    casts = iter(range(NHC))

    def cast_head(times):
        for _ in range(times):
            k = next(casts, None)
            if k is None:
                return
            if k + 1 < NHC:
                fetch_head(k + 1, True)
            fetch_head(k, False)
            m = HC if k < NHC - 1 else COLS - (NHC - 1) * HC
            u = 128 if m % 128 == 0 else 112

            def one(i, carry, k=k, u=u):
                rs = pl.ds(pl.multiple_of(i * u, 16), u)
                head_ref[pl.ds(pl.multiple_of(k * HC + i * u, 16), u), :] = hbuf[k % 2, rs, :].astype(jnp.bfloat16)
                return carry
            lax.fori_loop(0, m // u, one, 0)

    for a in (MISC, W_IN, W_MID):
        gath.begin(a)
    for r in range(SIDE):
        if r + 1 < SIDE:
            fetch_frames(r + 1).start()
        fetch_frames(r).wait()
        v = fbuf[r % 2].astype(jnp.float32).reshape(VR, D)
        x_ref[r * RB:(r + 1) * RB, :] = jnp.concatenate([v, jnp.zeros((TB, D), jnp.float32)], axis=0).astype(jnp.bfloat16)
    clear_margins(e_ref, o_ref)
    head_ref[COLS:PADC, :] = jnp.zeros((PADC - COLS, 128), jnp.bfloat16)
    far = n // 4 - 1
    kept = [pltpu.make_async_copy(src, dst, k_sem.at[k]) for k, (src, dst) in enumerate((
        (x_ref, x_hbm), (h1_ref, h1_hbm), (a2_ref, a2_hbm), (dh3_ref, dh3_hbm), (e_ref, e_hbm), (o_ref, o_hbm),
        (wmid_ref, wmid_hbm)))]

    def keep(k):
        pl.when(role == 0)(kept[k].start)
    keep(0)

    def z_step(a, d):
        if d <= far:
            gath.along_z(a, d)

    def x_step(a, d):
        if d <= far:
            gath.along_x(a, d)
    for d in range(1, far + 1):
        z_step(W_IN, d)
        z_step(MISC, d)
        cast_head(2)
        x_step(W_IN, d - 1)
        x_step(MISC, d - 1)
        z_step(W_MID, d)
        cast_head(2)
        if d == max(far - 1, 1):
            gath.begin(W_OUT)
    x_step(W_IN, far)
    x_step(MISC, far)
    x_step(W_MID, 0)
    x_step(W_MID, 1)
    cast_head(1)
    z_step(W_OUT, 1)
    gath.arrived(MISC)
    gath.arrived(W_IN)
    for i in range(n):
        gall_ref[i] = misc_ref[i, TB:2 * TB, :]
        for k in range(3):
            at = (i * 3 + k) * 128
            g_ref[:, at:at + 128] = misc_ref[i, k:k + 1, :]

    def mm1(i, carry):
        rs = pl.ds(pl.multiple_of(i * BLK, BLK), BLK)
        h1_ref[rs, :] = jnp.dot(x_ref[rs, :], win_ref[...], preferred_element_type=jnp.float32)
        return carry
    lax.fori_loop(0, ROWS // BLK, mm1, 0)
    z_step(W_OUT, 2)
    x_step(W_MID, 2)
    keep(1)
    mean, rstd = moments(h1_ref, 0, MID // GROUPS)
    st_ref[0:8, 0:MID] = mean
    st_ref[8:16, 0:MID] = rstd
    sc = rstd * g_ref[:, 0:MID]
    sh = g_ref[:, MID:2 * MID] - mean * sc

    def act1(r, carry):
        h = h1_ref[row_at(r), :].reshape(SIDE, TB, MID)
        a = gelu(h * sc[None] + sh[None]).reshape(VR, MID)
        put_shifted(e_ref, o_ref, r, a)
        return carry
    lax.fori_loop(0, SIDE, act1, 0)
    inner = pl.ds(PAD, ROWS)

    def far_a1(to):
        return rc(e_ref.at[inner], far_ref, ss.at[0], rs_.at[0], {"role": to})

    pl.when(role == 0)(lambda: far_a1(1).start())
    cast_head(NHC)
    z_step(W_OUT, 3)
    for d in range(3, far + 1):
        x_step(W_MID, d)
    gath.arrived(W_MID)
    keep(6)

    def mm2(i, carry):
        row = i * BLK
        acc = None
        for m, s in enumerate(OFFS):
            p = jnp.dot(shifted(e_ref, o_ref, s, row, BLK), wmid_ref[m * MID:(m + 1) * MID, :],
                        preferred_element_type=jnp.float32)
            acc = p if acc is None else acc + p
        h2_ref[pl.ds(pl.multiple_of(row, BLK), BLK), :] = acc
        return carry
    lax.fori_loop(0, ROWS // BLK, mm2, 0)
    for d in range(far + 1):
        x_step(W_OUT, d)
    mean, rstd = moments(h2_ref, 0, MID // GROUPS)
    st_ref[0:8, MID:2 * MID] = mean
    st_ref[8:16, MID:2 * MID] = rstd
    sc2 = rstd * g_ref[:, 2 * MID:3 * MID]
    sh2 = g_ref[:, 3 * MID:4 * MID] - mean * sc2

    def act2(r, carry):
        h = h2_ref[rows_full(r), :].reshape(PITCH, TB, MID)
        a2_ref[rows_full(r), :] = gelu(h * sc2[None] + sh2[None]).reshape(RB, MID).astype(jnp.bfloat16)
        return carry
    lax.fori_loop(0, SIDE, act2, 0)
    keep(2)
    gath.arrived(W_OUT)

    def mm3(i, carry):
        rs = pl.ds(pl.multiple_of(i * BLK, BLK), BLK)
        h3_ref[rs, :] = jnp.dot(a2_ref[rs, :], wout_ref[...], preferred_element_type=jnp.float32)
        return carry
    lax.fori_loop(0, ROWS // BLK, mm3, 0)
    for k in range(D // CH):
        lo = k * CH
        mean, rstd = moments(h3_ref, lo, D // GROUPS)
        st_ref[0:8, 2 * MID + lo:2 * MID + lo + CH] = mean
        st_ref[8:16, 2 * MID + lo:2 * MID + lo + CH] = rstd
        sc3 = rstd * g_ref[:, 4 * MID + lo:4 * MID + lo + CH]
        sh3 = g_ref[:, 4 * MID + D + lo:4 * MID + D + lo + CH] - mean * sc3

        def act3(r, acc):
            h = h3_ref[row_at(r), lo:lo + CH].reshape(SIDE, TB, CH)
            s = x_ref[rows_full(r), lo:lo + CH].astype(jnp.float32)[0:VR].reshape(SIDE, TB, CH)
            return acc + jnp.sum(gelu(s + (h * sc3[None] + sh3[None])), axis=0)
        acc = lax.fori_loop(0, SIDE, act3, jnp.zeros((TB, CH), jnp.float32))
        feat = (acc / float(PIX)).astype(jnp.bfloat16).astype(jnp.float32)
        for j in range(lo // 128, (lo + CH) // 128):
            fsend[j] = feat[:, j * 128 - lo:(j + 1) * 128 - lo]

            @pl.when(me != j)
            def _(j=j):
                rc(fsend.at[j], frecv.at[me], s_f.at[j], q_f.at[me], {"dp": j}).start()

            @pl.when(me == j)
            def _(j=j):
                frecv[j] = fsend[j]

    z8 = jnp.zeros((TB, CH), jnp.float32)

    def slopes(k):
        lo = k * CH
        cs = slice(lo, lo + CH)
        mean = st_ref[0:8, 2 * MID + lo:2 * MID + lo + CH]
        rstd = st_ref[8:16, 2 * MID + lo:2 * MID + lo + CH]
        gain = g_ref[:, 4 * MID + lo:4 * MID + lo + CH]
        shift = g_ref[:, 4 * MID + D + lo:4 * MID + D + lo + CH]
        mr = mean * rstd

        def one(r, acc):
            s1, s2 = acc
            h = h3_ref[row_at(r), cs].reshape(SIDE, TB, CH)
            v = x_ref[rows_full(r), cs].astype(jnp.float32)[0:VR].reshape(SIDE, TB, CH)
            xh = h * rstd[None] - mr[None]
            t = dgelu(v + (xh * gain + shift))
            dh3_ref[rows_full(r), cs] = jnp.concatenate([t.reshape(VR, CH), z8], axis=0).astype(jnp.bfloat16)
            return s1 + jnp.sum(t, axis=0), s2 + jnp.sum(t * xh, axis=0)
        s1, s2 = lax.fori_loop(0, SIDE, one, (z8, z8))
        sl_ref[0:8, cs] = s1
        sl_ref[8:16, cs] = s2

    @pl.when(role == 0)
    def _():
        slopes(0)
        slopes(1)
    for p in peers:
        rc(fsend.at[p], frecv.at[p], s_f.at[0], q_f.at[p], {"dp": p}).wait_recv()
    feats = frecv[...].reshape(n * TB, 128)
    ids = gall_ref[...].reshape(n * TB, 128).astype(jnp.int32)

    acc = None
    def two_windows(i):
        a, b = window_of(i), window_of(i + 1)
        return jnp.concatenate([head_ref[a:a + WIN, :], head_ref[b:b + WIN, :]], axis=1)
    for i in range(0, GAMES, 2):
        lhs = jnp.concatenate([jnp.where(ids == i, feats, 0.0), jnp.where(ids == i + 1, feats, 0.0)], axis=1)
        p = lax.dot_general(lhs.astype(jnp.bfloat16), two_windows(i), T1, preferred_element_type=jnp.float32)
        acc = p if acc is None else acc + p
    off = ids_offset(ids)
    part[...] = shift_rows(acc, off, False).reshape(half, 2, TB, LW)

    d1 = rc(part.at[:, 1 - c], r1, s_1, q_1, {"dp": cp})
    d1.start()
    d1.wait()
    pair = me // 2
    r1[...] = r1[...] + part[:, c]
    pps = [lax.rem(pair + k, half) for k in range(1, half)]
    for k, p in enumerate(pps):
        rc(r1.at[p], r2.at[pair], s_2.at[k], q_2.at[pair], {"dp": 2 * p + c}).start()
    r2[pair] = r1[pair]

    @pl.when(role == 0)
    def _():
        slopes(2)
        slopes(3)
    for k, p in enumerate(pps):
        rc(r1.at[p], r2.at[p], s_2.at[k], q_2.at[p], {"dp": 2 * p + c}).wait_recv()
    logits = jnp.sum(r2[...], axis=0)

    lane = lax.broadcasted_iota(jnp.int32, (TB, 128), 1)
    live = lane < ATOMS
    zi = support_low + (support_high - support_low) * lane.astype(jnp.float32) / (ATOMS - 1)
    zi = jnp.where(live, zi, 0.0)
    taken, nxt, expert, reward, done, gid = (scal_ref[k] for k in range(6))
    pieces = []
    for a in range(ACTIONS):
        v = logits if a == 0 else pltpu.roll(logits, LW - ATOMS * a, 1)
        pieces.append(v[:, :128])

    @pl.when(role == 1)
    def _():
        sel = jnp.zeros((TB, 128), jnp.float32)
        for a in range(ACTIONS):
            sel = sel + jnp.where(nxt == float(a), pieces[a], 0.0)
        sel = jnp.where(live, sel, -1e30)
        e = jnp.exp(sel - jnp.max(sel, axis=1, keepdims=True))
        e = jnp.where(live, e, 0.0)
        prob = e / jnp.sum(e, axis=1, keepdims=True)
        spacing = (support_high - support_low) / (ATOMS - 1)
        m = jnp.zeros((TB, 128), jnp.float32)
        for j in range(ATOMS):
            zj = float(np.float32(support_low) + np.float32(support_high - support_low) * np.float32(j) /
                       np.float32(ATOMS - 1))
            tz = jnp.clip(reward + discount * (1.0 - done) * zj, support_low, support_high)
            wt = jnp.maximum(0.0, 1.0 - jnp.abs(tz - zi) / spacing)
            m = m + prob[:, j:j + 1] * wt
        tgt_s[...] = jnp.where(live, m, 0.0)
        d = rc(tgt_s, tgt_r, s_t, q_t, {"role": 0})
        d.start()
        d.wait_send()
        rc(frow_ref, frow_ref, s_r.at[0], q_r.at[0], {"role": 0}).wait_recv()
        rc(dlog_ref, dlog_ref, s_r.at[1], q_r.at[1], {"role": 0}).wait_recv()
        dfeat_ref[...] = jnp.zeros_like(dfeat_ref)

    @pl.when(role == 0)
    def _():
        frow_ref[...] = feats.astype(jnp.bfloat16)
        gt = jnp.transpose(gall_ref[...].reshape(n * TB, 128))[0:TB]
        count = jnp.sum((gt == gid).astype(jnp.float32), axis=1, keepdims=True)
        weight = 1.0 / jnp.maximum(count, 1.0)
        x3 = jnp.where(live[None], jnp.stack(pieces), -1e30)
        act = lax.broadcasted_iota(jnp.int32, (ACTIONS, TB, 128), 0).astype(jnp.float32)
        hot = (act == taken[None]).astype(jnp.float32)
        mx = jnp.max(x3, axis=2, keepdims=True)
        e = jnp.where(live[None], jnp.exp(x3 - mx), 0.0)
        s = jnp.sum(e, axis=2, keepdims=True)
        logp = jnp.where(live[None], x3 - mx - jnp.log(s), 0.0)
        prob = e / s
        q = jnp.sum(prob * zi[None], axis=2, keepdims=True)
        qb = jnp.broadcast_to(q, (ACTIONS, TB, 128))
        qm = jnp.max(qb, axis=0)
        qe = jnp.exp(qb - qm[None])
        qs = jnp.sum(qe, axis=0)
        lse = qm + jnp.log(qs)
        pol = qe / qs[None]
        chosen = jnp.sum(logp * hot, axis=0)
        qt = jnp.sum(qb * hot, axis=0)
        rc(tgt_s, tgt_r, s_t, q_t, {"role": 1}).wait_recv()
        m = tgt_r[...]
        cross = -jnp.sum(m * chosen, axis=1, keepdims=True)
        row_loss = cross + penalty * expert * (lse - qt)
        msum = jnp.sum(m, axis=1, keepdims=True)
        dl = hot * (prob * msum[None] - m[None]) + (penalty * expert)[None] * (pol - hot) * prob * (zi[None] - qb)
        dl = jnp.where(live[None], dl * (weight * (1.0 / GAMES))[None], 0.0)
        flat = jnp.zeros((TB, LW), jnp.float32)
        pad = jnp.zeros((TB, LW - 128), jnp.float32)
        for a in range(ACTIONS):
            v = jnp.concatenate([dl[a], pad], axis=1)
            flat = flat + (v if a == 0 else pltpu.roll(v, ATOMS * a, 1))
        l0 = row_loss * weight
        p0 = l0.astype(jnp.bfloat16).astype(jnp.float32)
        p1 = (l0 - p0).astype(jnp.bfloat16).astype(jnp.float32)
        p2 = l0 - p0 - p1
        last = flat[:, LW - 128:]
        last = jnp.where(lane == 125, p0, jnp.where(lane == 126, p1, jnp.where(lane == 127, p2, last)))
        flat = jnp.concatenate([flat[:, :LW - 128], last], axis=1)
        down_s[...] = jnp.concatenate([flat[:, :LW // 2], flat[:, LW // 2:]], axis=0).astype(jnp.bfloat16)
        for k, p in enumerate(pps):
            rc(down_s, dlog_ref.at[me], s_l.at[k], q_l.at[me], {"dp": 2 * p + c}).start()
        rc(down_s, dlog_ref.at[me], s_c.at[0], q_c.at[me], {"dp": cp}).start()
        dlog_ref[me] = down_s[...]
        for k, p in enumerate(pps):
            o = 2 * p + c
            rc(down_s, dlog_ref.at[o], s_l.at[k], q_l.at[o], {"dp": cp}).wait_recv()
            rc(dlog_ref.at[o], dlog_ref.at[o], s_c.at[k + 1], q_c.at[o], {"dp": cp}).start()
        for p in [pair] + pps:
            o = 2 * p + 1 - c
            rc(dlog_ref.at[o], dlog_ref.at[o], s_c.at[0], q_c.at[o], {"dp": cp}).wait_recv()
        to0 = rc(frow_ref, frow_ref, s_r.at[0], q_r.at[0], {"role": 1})
        to1 = rc(dlog_ref, dlog_ref, s_r.at[1], q_r.at[1], {"role": 1})
        to0.start()
        to1.start()
        rolled = shift_rows(widen(dlog_ref[...]), off, True).astype(jnp.bfloat16)
        acc = None
        for i in range(0, GAMES, 2):
            p = jnp.dot(rolled, two_windows(i), preferred_element_type=jnp.float32)
            p = jnp.where(ids == i, p[:, :128], jnp.where(ids == i + 1, p[:, 128:], 0.0))
            acc = p if acc is None else acc + p
        dsend[...] = acc.reshape(n, TB, 128)
        for k, p in enumerate(peers):
            rc(dsend.at[p], drecv.at[me], s_d.at[k], q_d.at[me], {"dp": p}).start()
        drecv[me] = dsend[me]
        for k, p in enumerate(peers):
            rc(dsend.at[p], drecv.at[p], s_d.at[k], q_d.at[p], {"dp": p}).wait_recv()
        for j in range(n):
            dfeat_ref[:, j * 128:(j + 1) * 128] = drecv[j]
        for k, p in enumerate(pps):
            rc(down_s, dlog_ref.at[me], s_l.at[k], q_l.at[me], {"dp": 2 * p + c}).wait_send()
        rc(down_s, dlog_ref.at[me], s_c.at[0], q_c.at[me], {"dp": cp}).wait_send()
        for k, p in enumerate(pps):
            o = 2 * p + c
            rc(dlog_ref.at[o], dlog_ref.at[o], s_c.at[k + 1], q_c.at[o], {"dp": cp}).wait_send()
        for k, p in enumerate(peers):
            rc(dsend.at[p], drecv.at[me], s_d.at[k], q_d.at[me], {"dp": p}).wait_send()
        to0.wait_send()
        to1.wait_send()

    for j in range(n):
        pl.when(me != j)(rc(fsend.at[j], frecv.at[me], s_f.at[j], q_f.at[me], {"dp": j}).wait_send)
    for k, p in enumerate(pps):
        rc(r1.at[p], r2.at[pair], s_2.at[k], q_2.at[pair], {"dp": 2 * p + c}).wait_send()
    tail = dlog_ref[:, :, 384:512].astype(jnp.float32)[:, TB:2 * TB].reshape(n * TB, 128)
    lanes = lax.broadcasted_iota(jnp.int32, (n * TB, 128), 1)
    total = jnp.sum(jnp.where(lanes >= 125, tail, 0.0))
    loss_ref[...] = jnp.full((TB, 128), total, jnp.float32)

    def last_norm():
        for k in range(D // CH):
            lo = k * CH
            cs = slice(lo, lo + CH)
            mean = st_ref[0:8, 2 * MID + lo:2 * MID + lo + CH]
            rstd = st_ref[8:16, 2 * MID + lo:2 * MID + lo + CH]
            gain = g_ref[:, 4 * MID + lo:4 * MID + lo + CH]
            dout = dfeat_ref[:, cs] / float(PIX)
            s1 = dout * sl_ref[0:8, cs]
            s2 = dout * sl_ref[8:16, cs]
            put_gain(gg_ref, 4 * MID + lo, s2)
            put_gain(gg_ref, 4 * MID + D + lo, s1)
            count = 1.0 / float(PIX * D // GROUPS)
            m1 = group_sum(gain * s1, D // GROUPS) * count
            m2 = group_sum(gain * s2, D // GROUPS) * count
            cc = -rstd * rstd * m2
            cb = -rstd * m1 - mean * cc
            ca = rstd * gain * dout

            def one(r, carry):
                h = h3_ref[row_at(r), cs].reshape(SIDE, TB, CH)
                t = dh3_ref[rows_full(r), cs].astype(jnp.float32)[0:VR].reshape(SIDE, TB, CH)
                v = (ca[None] * t + cc[None] * h + cb[None]).reshape(VR, CH)
                dh3_ref[rows_full(r), cs] = jnp.concatenate([v, z8], axis=0).astype(jnp.bfloat16)
                return carry
            lax.fori_loop(0, SIDE, one, 0)

    @pl.when(role == 0)
    def _():
        last_norm()
        kept[3].start()

        def da2(i, c):
            rs = pl.ds(pl.multiple_of(i * BLK, BLK), BLK)
            d2_ref[rs, :] = lax.dot_general(dh3_ref[rs, :], wout_ref[...], T1, preferred_element_type=jnp.float32)
            return c
        lax.fori_loop(0, ROWS // BLK, da2, 0)
        far_a1(1).wait_send()
        through(h2_ref, d2_ref, st_ref, g_ref, gg_ref, MID, 2 * MID, 3 * MID,
                lambda r, v: put_shifted(e_ref, o_ref, r, v))
        kept[4].start()
        kept[5].start()
        gg_ref[:, 0:2 * MID] = jnp.zeros((1, 2 * MID), jnp.float32)
        for d in kept:
            d.wait()

    @pl.when(role == 1)
    def _():
        far_a1(0).wait_recv()
        for k in range(MID // 128):
            fart_ref[k * 128:(k + 1) * 128, :] = jnp.transpose(far_ref[:, k * 128:(k + 1) * 128])
        d = pltpu.make_async_copy(fart_ref, fart_hbm, k_sem.at[7])
        d.start()
        d.wait()
        gg_ref[...] = jnp.zeros_like(gg_ref)
    gath.end()


def block_step(frames, weights, averages, scal, head, avg_head, n, cid):
    f32, b16 = jnp.float32, jnp.bfloat16
    S = jax.ShapeDtypeStruct
    V, dma = pltpu.VMEM, pltpu.SemaphoreType.DMA
    vs, hs = pl.BlockSpec(memory_space=pltpu.VMEM), pl.BlockSpec(memory_space=pl.ANY)
    h = n // 2
    nz = n // 4
    sends = 4 + 6 * (nz - 1) + 2 * nz
    return pl.pallas_call(
        functools.partial(step_kernel, n),
        out_shape=(S((ROWS, D), b16), S((ROWS, MID), f32), S((ROWS, MID), b16), S((ROWS, D), b16), S((EROWS, MID), b16),
                   S((EROWS, MID), b16), S((9 * MID, MID), b16), S((MID, ROWS), b16), S((16, 2 * MID + D), f32),
                   S((1, 4 * MID + 2 * D), f32), S((1, 4 * MID + 2 * D), f32), S((n, TB, 128), f32), S((n * TB, 128), b16), S((n, 16, 512), b16), S((TB, 128), f32)),
        in_specs=[hs] + [vs] * 8 + [pl.BlockSpec(memory_space=pltpu.SMEM)] * 6 + [hs] * 2,
        out_specs=(hs,) * 8 + (vs,) * 7,
        scratch_shapes=[
            V((6, TB, 128), f32), V((D // n, MID), b16), V((9 * MID // n, MID), b16), V((MID // n, D), b16), V((16, 128), f32),
            V((D, MID), b16), V((9 * MID, MID), b16), V((MID, D), b16), V((n, 16, 128), f32),
            V((ROWS, D), b16), V((ROWS, MID), f32), V((ROWS, MID), f32), V((ROWS, D), f32), V((ROWS, MID), b16),
            V((TB, D), f32), V((16, D), f32), V((EROWS, MID), b16), V((EROWS, MID), b16),
            V((ROWS, MID), f32), V((ROWS, D), b16), V((ROWS, MID), b16), V((MID, ROWS), b16),
            V((2, SIDE, TB, D), b16), V((2, HC, 128), f32), V((PADC, 128), b16),
            V((n, TB, 128), f32), V((n, TB, 128), f32), V((h, 2, TB, LW), f32), V((h, TB, LW), f32),
            V((h, TB, LW), f32), V((TB, 128), f32), V((TB, 128), f32), V((16, 512), b16),
            V((n, TB, 128), f32), V((n, TB, 128), f32),
            dma((4,)), dma((4, sends)), dma((4, n)), dma((2,)), dma((2,)), dma((8,)), dma((1,)), dma((1,)),
            dma((n,)), dma((n,)), dma, dma, dma((h,)), dma((h,)), dma, dma, dma((h,)), dma((n,)),
            dma((h,)), dma((n,)), dma((n,)), dma((n,)), dma((2,)), dma((2,))],
        compiler_params=pltpu.CompilerParams(collective_id=cid, has_side_effects=True,
                                             vmem_limit_bytes=64 * 1024 * 1024),
        name="block_step",
    )(frames, *weights, *averages, *scal, head, avg_head)


KEEP, SEND, BOTH = 0, 1, 2
OUT, MIDDLE, IN, GAINS = 0, 1, 2, 3


def units_of(ri, ro, rm):
    q, h, t = MID // 4, ri // 2, rm // 2
    online = ((0, ri + 2 * ro, 2 * ro, 0, MID, SEND, OUT), (0, ri, 2 * ro, 0, MID, KEEP, OUT),
              (0, 0, ri, MID // 2, MID // 2, SEND, IN), (0, 0, h, 0, MID // 2, KEEP, IN), (0, h, h, 0, MID // 2, KEEP, IN),
              (1, 0, 3, 0, 128, BOTH, GAINS))
    target = ((0, 0, rm, 0, q, SEND, MIDDLE), (0, 0, rm, q, q, SEND, MIDDLE), (0, 0, rm, 2 * q, q, KEEP, MIDDLE),
              (0, 0, t, 3 * q, q, KEEP, MIDDLE), (0, t, 96, 3 * q, q, KEEP, MIDDLE),
              (0, t + 96, t - 96, 3 * q, q, KEEP, MIDDLE))
    return online, target


def sums_kernel(n_dev, rows, x_hbm, h1_hbm, a2_hbm, dh3_hbm, e_hbm, o_hbm, wmid_hbm, fart_hbm, st_ref, g_ref, gpart_ref,
                gall_ref, frow_ref, dlog_ref, t_out, t_mid, t_in, t_gains, dlt, rhs, x_ref, h1_ref, a2_ref, dh3_ref, e_ref, o_ref, wmid_ref, fart_ref, low_ref,
                d2_ref, gg_ref, *refs):
    outs = (t_out, t_mid, t_in, t_gains)
    g, r1, r2, rz = (refs[2 * j:2 * j + 2] for j in range(4))
    fs, fr = refs[8:12], refs[12:16]
    s1, q1, s2, q2, s3, q3, sf, qf, sl, sd, qd = refs[16:]
    nz = n_dev // 4
    ri, ro, rm = rows
    online, target = units_of(*rows)
    me, z, x, c = place()
    role = lax.axis_index("role")
    xp = {"dp": me + 2 - 4 * x}
    cp = {"dp": me + 1 - 2 * c}

    def slot(zz, xx, cc):
        return zz * 4 + xx * 2 + cc

    order = list(range(nz))
    parts = ((0, 128), (128, 128), (256, 128), (384, MID - 384))

    def load(k):
        src = (x_hbm, h1_hbm, a2_hbm, dh3_hbm, e_hbm, o_hbm, wmid_hbm, fart_hbm)[k]
        dst = (x_ref, h1_ref, a2_ref, dh3_ref, e_ref, o_ref, wmid_ref, fart_ref)[k]
        return pltpu.make_async_copy(src, dst, sl.at[k])

    def far_d2(to, k):
        cs = pl.ds(*parts[k])
        return rc(e_hbm.at[pl.ds(PAD, ROWS), cs], low_ref.at[:, cs], sd.at[k], qd.at[k], {"role": to})

    @pl.when(role == 0)
    def _():
        for k in (3, 2, 6, 4, 5, 1, 0):
            load(k).start()
    pl.when(role == 1)(load(7).start)
    zs = [{"dp": lax.rem(me + 4 * k, 4 * nz)} for k in range(1, nz)]
    greet([(None, p) for p in [xp, cp, {"role": 1 - role}] + zs])
    z8 = jnp.zeros((TB, CH), jnp.float32)

    def online_first():
        for k in range(len(parts)):
            far_d2(1, k).start()
        gg_ref[...] = gpart_ref[...]
        load(3).wait()
        load(2).wait()
        for k in (2, 3, 0, 1):
            v = lax.dot_general(a2_ref[...], dh3_ref[:, k * CH:(k + 1) * CH], T0, preferred_element_type=jnp.float32)
            g[0][:, ri + k * ro:ri + (k + 1) * ro, :] = v.reshape(n_dev, ro, CH)

    def online_rest():
        for k in (6, 4, 5, 1, 0):
            load(k).wait()

        def da1(i, carry):
            row = i * BLK
            acc = None
            for m, s in enumerate(OFFS):
                p = lax.dot_general(shifted(e_ref, o_ref, -s, row, BLK), wmid_ref[m * MID:(m + 1) * MID, :], T1,
                                    preferred_element_type=jnp.float32)
                acc = p if acc is None else acc + p
            d2_ref[pl.ds(pl.multiple_of(row, BLK), BLK), :] = acc
            return carry
        lax.fori_loop(0, ROWS // BLK, da1, 0)

        def put1(r, v):
            low_ref[rows_full(r), :] = jnp.concatenate([v, z8], axis=0).astype(jnp.bfloat16)
        through(h1_ref, d2_ref, st_ref, g_ref, gg_ref, 0, 0, MID, put1)
        per = CH // ri
        for k in range(D // CH):
            v = lax.dot_general(x_ref[:, k * CH:(k + 1) * CH], low_ref[...], T0, preferred_element_type=jnp.float32)
            g[0][k * per:(k + 1) * per, 0:ri, :] = v.reshape(per, ri, MID)
        for i in range(n_dev):
            for k in range(3):
                at = (i * 3 + k) * 128
                g[1][i, k:k + 1, :] = gg_ref[:, at:at + 128]

    def target_part(k):
        if k == 0:
            clear_margins(e_ref, o_ref)
            load(7).wait()
        cs = slice(parts[k][0], parts[k][0] + parts[k][1] if k < 2 else MID)
        far_d2(0, k).wait_recv()
        if k == 2:
            far_d2(0, 3).wait_recv()
        zh = jnp.zeros((TB, cs.stop - cs.start), jnp.float32)

        def rebuild(r, carry):
            v = low_ref[rows_full(r), cs].astype(jnp.float32)
            at = pl.ds(pl.multiple_of(PAD + r * RB, 16), RB)
            e_ref[at, cs] = low_ref[rows_full(r), cs]
            o_ref[at, cs] = jnp.concatenate([zh, v[0:VR]], axis=0).astype(jnp.bfloat16)
            return carry
        lax.fori_loop(0, SIDE, rebuild, 0)
        for m, s in enumerate(OFFS):
            ref, base = (e_ref, 16 - s) if s % 2 == 0 else (o_ref, 17 - s)
            v = jnp.dot(fart_ref[...], ref[base * TB:base * TB + ROWS, cs], preferred_element_type=jnp.float32)
            at = m * MID
            while at < (m + 1) * MID:
                i = at // rm
                end = min((i + 1) * rm, (m + 1) * MID)
                g[0][i, at - i * rm:end - i * rm, cs] = v[at - m * MID:end - m * MID]
                at = end

    def cut(ref, i, u):
        return ref.at[i, pl.ds(u[1], u[2]), pl.ds(u[3], u[4])]

    def region(u):
        if u[6] == OUT:
            return slice(0, ro), slice(0, outs[OUT].shape[1])
        at = u[3] % outs[u[6]].shape[1]
        return slice(u[1], u[1] + u[2]), slice(at, at + u[4])

    def place_sum(u, total):
        if u[6] == OUT:
            return jnp.concatenate([total[j * ro:(j + 1) * ro] for j in range(u[2] // ro)], axis=1)
        return total

    def final(u, to, n):
        rs, cs = region(u)
        at = (pl.ds(rs.start, rs.stop - rs.start), pl.ds(cs.start, cs.stop - cs.start))
        return rc(fs[u[6]].at[at], fr[u[6]].at[at], sf.at[n], qf.at[n], {"role": to})

    def run(units, mine, plan):
        def add(u, i, ref, j):
            a, rs, cs = u[0], slice(u[1], u[1] + u[2]), slice(u[3], u[3] + u[4])
            g[a][i, rs, cs] = g[a][i, rs, cs] + ref[a][j, rs, cs]

        def c1(n, zz, k):
            u = units[n]
            xx = 1 - x if k == 0 else x
            return rc(cut(g[u[0]], slot(zz, xx, 1 - c), u), cut(r1[u[0]], k * nz + zz, u), s1.at[n, k * nz + zz],
                      q1.at[n, k * nz + zz], cp)

        def c2(n, zz):
            u = units[n]
            return rc(cut(g[u[0]], slot(zz, 1 - x, c), u), cut(r2[u[0]], zz, u), s2.at[n, zz], q2.at[n, zz], xp)

        def c3(n, t, at):
            u = units[n]
            return rc(cut(g[u[0]], slot(t, x, c), u), cut(rz[u[0]], at, u), s3.at[n, t], q3.at[n, at],
                      {"dp": slot(t, x, c)})

        def gather_x(n):
            u = units[n]
            for zz in order:
                c1(n, zz, 1).wait_recv()
                add(u, slot(zz, x, c), r1, nz + zz)
            for zz in order:
                c2(n, zz).wait_recv()
                add(u, slot(zz, x, c), r2, zz)
                pl.when(z != zz)(c3(n, zz, z).start)

        def first(n):
            for k in range(2):
                for zz in order:
                    c1(n, zz, k).start()

        def second(n):
            for zz in order:
                c1(n, zz, 0).wait_recv()
                add(units[n], slot(zz, 1 - x, c), r1, zz)
                c2(n, zz).start()

        def finish(n):
            u = units[n]
            a, rs, cs = u[0], slice(u[1], u[1] + u[2]), slice(u[3], u[3] + u[4])
            for zz in order:
                @pl.when(z != zz)
                def _(zz=zz):
                    c3(n, z, zz).wait_recv()
                    add(u, me, rz, zz)
            total = place_sum(u, g[a][me, rs, cs])
            at = region(u)
            if u[5] != SEND:
                outs[u[6]][at] = total
            if u[5] != KEEP:
                fs[u[6]][at] = total.astype(fs[u[6]].dtype)
                final(u, 1 - mine, n).start()
        def operands():
            ids = gall_ref[...].reshape(-1, 128).astype(jnp.int32) - mine * (GAMES // 2)
            v = shift_rows(widen(dlog_ref[...]), ids_offset(ids), True)
            for k in range(WIN // 128):
                dlt[k * 128:(k + 1) * 128, :] = jnp.transpose(v[:, k * 128:(k + 1) * 128]).astype(jnp.bfloat16)
            feats = frow_ref[...].astype(jnp.float32)
            for i in range(GAMES // 2):
                rhs[i] = jnp.where(ids == i, feats, 0.0).astype(jnp.bfloat16)

        def terms(ns):
            for n in ns:
                first(n)
            for n in ns:
                second(n)
        for do, what in plan:
            if do == "make":
                what()
            elif do == "head":
                operands()
            else:
                {"start": terms, "x": gather_x, "end": finish}[do](what)
        for n, u in enumerate(units):
            for zz in order:
                c1(n, zz, 0).wait_send()
                c1(n, zz, 1).wait_send()
                c2(n, zz).wait_send()
                pl.when(z != zz)(c3(n, zz, z).wait_send)
            if u[5] != KEEP:
                final(u, 1 - mine, n).wait_send()

    def receive(units, other):
        for n, u in enumerate(units):
            if u[5] != KEEP:
                final(u, other, n).wait_recv()
                outs[u[6]][region(u)] = fr[u[6]][region(u)].astype(jnp.float32)

    rest = [("x", 0), ("x", 1), ("x", 2), ("end", 0), ("x", 3), ("end", 1), ("x", 4), ("end", 2), ("x", 5), ("end", 3),
            ("end", 4), ("end", 5)]

    @pl.when(role == 0)
    def _():
        run(online, 0, [("make", online_first), ("start", (0, 1)), ("make", online_rest), ("start", (2, 3, 4, 5)), ("head", 0)] + rest)
        receive(target, 1)
        for k in range(len(parts)):
            far_d2(1, k).wait_send()

    @pl.when(role == 1)
    def _():
        run(target, 1, [("make", lambda: target_part(0)), ("start", (0,)), ("make", lambda: target_part(1)), ("start", (1,)),
                        ("x", 0), ("make", lambda: target_part(2)), ("start", (2, 3, 4, 5)), ("head", 0)] + rest[1:])
        receive(online, 0)


def sums(saved, games_all, frow, dlog, n, cid):
    nz = n // 4
    V, dma = pltpu.VMEM, pltpu.SemaphoreType.DMA
    f32, b16 = jnp.float32, jnp.bfloat16
    S = jax.ShapeDtypeStruct
    rows = ri, ro, rm = D // n, MID // n, 9 * MID // n
    half = [(ro, D // 2), (rm, MID // 2), (ri, MID // 2), (3, 128)]
    low = [b16, b16, b16, f32]
    sh = [(rm, MID), (3, 128)]
    nu = max(len(u) for u in units_of(*rows))
    vs, hs = pl.BlockSpec(memory_space=pltpu.VMEM), pl.BlockSpec(memory_space=pl.ANY)
    return pl.pallas_call(
        functools.partial(sums_kernel, n, rows),
        out_shape=tuple(S(s, f32) for s in half) + (S((WIN, n * TB), b16), S((GAMES // 2, n * TB, 128), b16)),
        in_specs=[hs] * 8 + [vs] * 6,
        out_specs=(vs,) * 6,
        scratch_shapes=[V(s.shape, s.dtype) for s in saved[:8]] +
        [V((ROWS, MID), b16), V((ROWS, MID), f32), V((1, 4 * MID + 2 * D), f32)] +
        [V((k,) + s, f32) for k in (4 * nz, 2 * nz, nz, nz) for s in sh] + [V(s, t) for s, t in zip(half, low)] * 2 +
        [dma((nu, 2 * nz))] * 2 + [dma((nu, nz))] * 4 + [dma((nu,))] * 2 + [dma((8,)), dma((4,)), dma((4,))],
        compiler_params=pltpu.CompilerParams(collective_id=cid, has_side_effects=True,
                                             vmem_limit_bytes=63 * 1024 * 1024),
        name="gradient_sums",
    )(*saved, games_all, frow, dlog)


UB = 2048
NU = -(-HALF // UB)
LASTU = HALF - (NU - 1) * UB


def segments(k):
    lo, hi = k * UB, min((k + 1) * UB, -(-HALF // 16) * 16)
    parts = []
    for i in range(GAMES // 2):
        a, end = window_of(i), window_of(i + 1)
        mixed = i > 0 and WIDE * i != a
        for r0, r1, games in ((a, a + 16, (i - 1, i)), (a + 16, end, (i,))) if mixed else ((a, end, (i,)),):
            if i == GAMES // 2 - 1 and r1 == end:
                r1 = -(-HALF // 16) * 16
            r0, r1 = max(r0, lo), min(r1, hi)
            if r0 < r1:
                parts.append((r0, r1, games))
    return parts


def update_kernel(dlt, rhs, loss_ref, *refs):
    grads, olds_hbm = refs[:4], refs[4:16]
    hbm = refs[16:19]
    loss_out, news, hbm_out = refs[19], refs[20:36], refs[36:40]
    olds = refs[40:52]
    grow, ibuf, obuf, cbuf, si, so, sw = refs[52:]
    role = lax.axis_index("role")

    def rows_of(k):
        return UB if k < NU - 1 else LASTU

    def fetch(k):
        n = rows_of(k)
        return [pltpu.make_async_copy(hbm[t].at[pl.ds(pl.multiple_of(role * HALF + k * UB, 8), n)],
                                      ibuf.at[k % 3, t, pl.ds(0, n)], si.at[k % 3, t]) for t in range(3)]

    def store(k):
        n = rows_of(k)
        cs = [pltpu.make_async_copy(obuf.at[k % 2, t, pl.ds(0, n)], hbm_out[t].at[pl.ds(k * UB, n)], so.at[k % 2, t])
              for t in range(3)]
        return cs + [pltpu.make_async_copy(cbuf.at[k % 2, pl.ds(0, n)], hbm_out[3].at[pl.ds(k * UB, n)], so.at[k % 2, 3])]

    old_copies = [pltpu.make_async_copy(olds_hbm[i], olds[i], sw.at[i]) for i in range(12)]
    for d in fetch(0) + fetch(1) + old_copies:
        d.start()
    loss_out[...] = loss_ref[0:1, 0:1]

    def small(a, right):
        w, m, v = olds[3 * a:3 * a + 3]
        nw, nm, nv, nc = news[4 * a:4 * a + 4]
        cols = grads[a].shape[1]
        cs = slice(cols if right else 0, (cols if right else 0) + cols)
        gv = grads[a][...]
        rate = learn_rate
        if a == 3:
            gv = jnp.concatenate([gv[k:k + 1, :] for k in range(gv.shape[0])], axis=1)
            cs = slice(0, gv.shape[1])
            rate = gain_rate
        mv = momentum_decay * m[:, cs] + gv
        wv = w[:, cs] - rate * (gv + momentum_decay * mv)
        nw[...] = wv
        nm[...] = gv if a == 0 else mv
        nv[...] = average_decay * v[:, cs] + (1.0 - average_decay) * wv
        nc[...] = wv.astype(jnp.bfloat16)

    for k in range(NU):
        if k + 2 < NU:
            for d in fetch(k + 2):
                d.start()
        lo = k * UB
        for r0, r1, games in segments(k):
            acc = None
            for i in games:
                at = r0 - window_of(i)
                p = jnp.dot(dlt[at:at + r1 - r0, :], rhs[i], preferred_element_type=jnp.float32)
                acc = p if acc is None else acc + p
            grow[r0 - lo:r1 - lo, :] = acc
        for d in fetch(k):
            d.wait()
        if k >= 2:
            for d in store(k - 2):
                d.wait()
        b, s = k % 2, k % 3

        def one(r, carry, b=b, s=s):
            rs = pl.ds(pl.multiple_of(r * 128, 128), 128)
            gv = grow[rs, :]
            m = momentum_decay * ibuf[s, 1, rs, :] + gv
            w = ibuf[s, 0, rs, :] - learn_rate * (gv + momentum_decay * m)
            obuf[b, 0, rs, :] = w
            obuf[b, 1, rs, :] = m
            obuf[b, 2, rs, :] = average_decay * ibuf[s, 2, rs, :] + (1.0 - average_decay) * w
            cbuf[b, rs, :] = w.astype(jnp.bfloat16)
            return carry
        lax.fori_loop(0, UB // 128, one, 0)
        for d in store(k):
            d.start()
        if 4 <= k < 8:
            a = k - 4
            for i in range(3 * a, 3 * a + 3):
                old_copies[i].wait()
            if a == 3:
                small(a, False)
            else:
                pl.when(role == 0)(lambda a=a: small(a, False))
                pl.when(role != 0)(lambda a=a: small(a, True))
    for k in (NU - 2, NU - 1):
        for d in store(k):
            d.wait()


def final_update(dlt, rhs, loss, grads, olds, tables):
    lanes = tables[0].shape[1]
    f32, b16 = jnp.float32, jnp.bfloat16
    S, V, dma = jax.ShapeDtypeStruct, pltpu.VMEM, pltpu.SemaphoreType.DMA
    vs, hs = pl.BlockSpec(memory_space=pltpu.VMEM), pl.BlockSpec(memory_space=pl.ANY)
    new_shapes = []
    for a in range(4):
        s = olds[3 * a].shape if a == 3 else grads[a].shape
        new_shapes += [S(s, f32)] * 3 + [S(s, b16)]
    return pl.pallas_call(
        update_kernel,
        in_specs=[vs] * 7 + [hs] * 15,
        out_specs=[vs] * 17 + [hs] * 4,
        scratch_shapes=[V(o.shape, f32) for o in olds] +
        [V((UB, lanes), f32), V((3, 3, UB, lanes), f32),
         V((2, 3, UB, lanes), f32), V((2, UB, lanes), b16), dma((3, 3)), dma((2, 4)), dma((12,))],
        out_shape=[S((1, 1), f32)] + new_shapes + [S((HALF, lanes), f32)] * 3 + [S((HALF, lanes), b16)],
        compiler_params=pltpu.CompilerParams(vmem_limit_bytes=63 * 1024 * 1024),
        name="final_update",
    )(dlt, rhs, loss, *grads, *olds, *tables)


def fast_device(
    frames,
    game_ids,
    taken_actions,
    next_actions,
    expert_flags,
    rewards,
    done_flags,
    weight_in,
    weight_mid,
    weight_out,
    norm_gains,
    head_table,
    moment_in,
    moment_mid,
    moment_out,
    moment_gains,
    moment_head,
    average_in,
    average_mid,
    average_out,
    average_gains,
    average_head,
):
    n = lax.axis_size("dp")
    *saved, all_ids, feat_rows, dlog, loss = block_step(
        jnp.transpose(frames[0], (1, 0, 2)),
        (weight_in[0], weight_mid[0], weight_out[0], norm_gains),
        (average_in[0], average_mid[0], average_out[0], average_gains),
        (taken_actions, next_actions, expert_flags, rewards, done_flags, game_ids),
        head_table.T,
        average_head.T,
        n,
        1,
    )
    grad_out, grad_mid, grad_in, grad_gains, dlt, rhs = sums(saved, all_ids, feat_rows, dlog, n, 2)
    loss, *rest = final_update(
        dlt,
        rhs,
        loss,
        (grad_in, grad_mid, grad_out, grad_gains),
        (
            weight_in[0],
            moment_in[0],
            average_in[0],
            weight_mid[0],
            moment_mid[0],
            average_mid[0],
            weight_out[0],
            moment_out[0],
            average_out[0],
            norm_gains,
            moment_gains,
            average_gains,
        ),
        (head_table.T, moment_head.T, average_head.T),
    )
    return (
        loss.reshape(()),
        *(v[None] for v in rest[:12]),
        *rest[12:16],
        *(v.T for v in rest[16:]),
    )


def solution(mesh):
    return jax.shard_map(
        fast_device if mesh.shape["dp"] == 16 else on_device,
        mesh=mesh,
        in_specs=(
            P("role", "dp", None, None),
            P("dp"),
            P("dp"),
            P("dp"),
            P("dp"),
            P("dp"),
            P("dp"),
            P(None, "dp", None),
            P(None, "dp", None),
            P(None, "dp", None),
            P(None, "dp"),
            P("dp", None),
            P(None, "dp", None),
            P(None, "dp", None),
            P(None, "dp", None),
            P(None, "dp"),
            P("dp", None),
            P(None, "dp", None),
            P(None, "dp", None),
            P(None, "dp", None),
            P(None, "dp"),
            P("dp", None),
        ),
        out_specs=(
            P(),
            P(None, "dp", "role"),
            P(None, "dp", "role"),
            P(None, "dp", "role"),
            P(None, "dp", "role"),
            P(None, "dp", "role"),
            P(None, "dp", "role"),
            P(None, "dp", "role"),
            P(None, "dp", "role"),
            P(None, "dp", "role"),
            P(None, "dp", "role"),
            P(None, "dp", "role"),
            P(None, "dp", "role"),
            P(None, "dp"),
            P(None, "dp"),
            P(None, "dp"),
            P(None, "dp"),
            P("dp", "role"),
            P("dp", "role"),
            P("dp", "role"),
            P("dp", "role"),
        ),
        check_vma=False,
    )
```

profile of v0, /device:TPU:6, one launch (start us, length us, event | category | flops | bytes accessed | tf_op | source)
XLA Modules:
  0.0 220.7 jit_solution(5732228154887477672)
XLA Ops:
  0.7 107.0 %block_step.1 = (bf16[1056,2048]{1,0:T(8,128)(2,1)}, f32[1056,512]{1,0:T(8,128)}, bf16[1056,512]{1,0:T(8,128)(2,1)}, bf16[1056,2048]{1,0:T(8,128)(2,1)}, bf16[13...) custom-call(bf16[121,8,2048]{2,1,0:T(8,128)(2,1)} %bitcast.37, ...), custom_call_target="tpu_custom_call" | custom-call | tf_op jit(solution)/shard_map/block_step/pallas_call | solution.py:1120
  107.7 88.6 %gradient_sums.1 = (f32[32,1024]{1,0:T(8,128)}, f32[288,256]{1,0:T(8,128)}, f32[128,256]{1,0:T(8,128)}, f32[3,128]{1,0:T(4,128)}, bf16[1024,128]{1,0:T(8,128)(2,1)}, /*index=5*/bf16[20,128,128]{2,1,0:T(8,128)(2,1)}) custom-call(bf16[1056,2048]{1,0:T(8,128)(2,1)} %get-tuple-element.63.x_hbm, f32[1056,512]{1,0:T(8,128)} %get-tuple-element.64.h1_hbm, ...), custom_call_target="tpu_custom_call" | custom-call | tf_op jit(solution)/shard_map/gradient_sums/pallas_call | solution.py:1403
  196.3 24.2 %final_update.1 = (f32[1,1]{1,0:T(1,128)}, f32[128,256]{1,0:T(8,128)}, f32[128,256]{1,0:T(8,128)}, f32[128,256]{1,0:T(8,128)}, bf16[128,256]{1,0:T(8,128)(2,1)},...) custom-call(bf16[1024,128]{1,0:T(8,128)(2,1)} %get-tuple-element.77., ...), custom_call_target="tpu_custom_call" | custom-call | tf_op jit(solution)/shard_map/final_update/pallas_call | solution.py:1538
where the time goes:
time: 222 us; the launch traced here: 221 us
  Pallas kernels  220 us (99%)
    pallas_call x1, Pallas kernels, block_step(): pl.pallas_call(functools.partial(step_kernel, n), out_shape=(S((ROWS, D),...  107 us
    pallas_call x1, Pallas kernels, sums(): pl.pallas_call(functools.partial(sums_kernel, n, rows), out_shape=tuple((...  88.6 us
    pallas_call x1, Pallas kernels, final_update(): pl.pallas_call(update_kernel, in_specs=[vs] * 7 + [hs] * 15, out_specs=[v...  24.2 us

commit v1 on v0

--- a/solution.py
+++ b/solution.py
@@ -1152,9 +1152,8 @@
     online = ((0, ri + 2 * ro, 2 * ro, 0, MID, SEND, OUT), (0, ri, 2 * ro, 0, MID, KEEP, OUT),
               (0, 0, ri, MID // 2, MID // 2, SEND, IN), (0, 0, h, 0, MID // 2, KEEP, IN), (0, h, h, 0, MID // 2, KEEP, IN),
               (1, 0, 3, 0, 128, BOTH, GAINS))
-    target = ((0, 0, rm, 0, q, SEND, MIDDLE), (0, 0, rm, q, q, SEND, MIDDLE), (0, 0, rm, 2 * q, q, KEEP, MIDDLE),
-              (0, 0, t, 3 * q, q, KEEP, MIDDLE), (0, t, 96, 3 * q, q, KEEP, MIDDLE),
-              (0, t + 96, t - 96, 3 * q, q, KEEP, MIDDLE))
+    target = ((0, 0, t, 0, q, SEND, MIDDLE), (0, t, t, 0, q, SEND, MIDDLE), (0, 0, rm, q, q, SEND, MIDDLE), (0, 0, rm, 2 * q, q, KEEP, MIDDLE),
+              (0, 0, rm, 3 * q, q, KEEP, MIDDLE))
     return online, target
 
 
@@ -1372,20 +1371,24 @@
                 final(u, other, n).wait_recv()
                 outs[u[6]][region(u)] = fr[u[6]][region(u)].astype(jnp.float32)
 
-    rest = [("x", 0), ("x", 1), ("x", 2), ("end", 0), ("x", 3), ("end", 1), ("x", 4), ("end", 2), ("x", 5), ("end", 3),
-            ("end", 4), ("end", 5)]
+    def rest(nu):
+        steps = [("x", 0), ("x", 1)]
+        for k in range(2, nu):
+            steps += [("x", k), ("end", k - 2)]
+        return steps + [("end", nu - 2), ("end", nu - 1)]
 
     @pl.when(role == 0)
     def _():
-        run(online, 0, [("make", online_first), ("start", (0, 1)), ("make", online_rest), ("start", (2, 3, 4, 5)), ("head", 0)] + rest)
+        run(online, 0, [("make", online_first), ("start", (0, 1)), ("make", online_rest), ("start", (2, 3, 4, 5)), ("head", 0)] + rest(6))
         receive(target, 1)
         for k in range(len(parts)):
             far_d2(1, k).wait_send()
 
     @pl.when(role == 1)
     def _():
-        run(target, 1, [("make", lambda: target_part(0)), ("start", (0,)), ("make", lambda: target_part(1)), ("start", (1,)),
-                        ("x", 0), ("make", lambda: target_part(2)), ("start", (2, 3, 4, 5)), ("head", 0)] + rest[1:])
+        run(target, 1, [("make", lambda: target_part(0)), ("start", (0, 1)), ("make", lambda: target_part(1)), ("x", 0),
+                        ("start", (2,)), ("x", 1), ("make", lambda: target_part(2)), ("start", (3, 4)),
+                        ("head", 0)] + rest(5)[2:])
         receive(online, 0)
 
 

time: 222 us -> 222 us (level); the launches traced: 221 us -> 218 us
  Pallas kernels: 220 us -> 217 us
    pallas_call x1, Pallas kernels: 88.6 us -> 85.8 us  [sums(): pl.pallas_call(functools.partial(sums_kernel, n, rows), out_shape=tuple((...]
where the time goes in v1:
time: 222 us; the launch traced here: 218 us
  Pallas kernels  217 us (98%)
    pallas_call x1, Pallas kernels, block_step(): pl.pallas_call(functools.partial(step_kernel, n), out_shape=(S((ROWS, D),...  107 us
    pallas_call x1, Pallas kernels, sums(): pl.pallas_call(functools.partial(sums_kernel, n, rows), out_shape=tuple((...  85.8 us
    pallas_call x1, Pallas kernels, final_update(): pl.pallas_call(update_kernel, in_specs=[vs] * 7 + [hs] * 15, out_specs=[v...  24.2 us

profile of v1, /device:TPU:6, one launch (start us, length us, event | category | flops | bytes accessed | tf_op | source)
XLA Modules:
  0.0 217.8 jit_solution(18280874759687251425)
XLA Ops:
  0.7 107.0 %block_step.1 = (bf16[1056,2048]{1,0:T(8,128)(2,1)}, f32[1056,512]{1,0:T(8,128)}, bf16[1056,512]{1,0:T(8,128)(2,1)}, bf16[1056,2048]{1,0:T(8,128)(2,1)}, bf16[13...) custom-call(bf16[121,8,2048]{2,1,0:T(8,128)(2,1)} %bitcast.37, ...), custom_call_target="tpu_custom_call" | custom-call | tf_op jit(solution)/shard_map/block_step/pallas_call | solution.py:1120
  107.7 85.8 %gradient_sums.1 = (f32[32,1024]{1,0:T(8,128)}, f32[288,256]{1,0:T(8,128)}, f32[128,256]{1,0:T(8,128)}, f32[3,128]{1,0:T(4,128)}, bf16[1024,128]{1,0:T(8,128)(2,1)}, /*index=5*/bf16[20,128,128]{2,1,0:T(8,128)(2,1)}) custom-call(bf16[1056,2048]{1,0:T(8,128)(2,1)} %get-tuple-element.63.x_hbm, f32[1056,512]{1,0:T(8,128)} %get-tuple-element.64.h1_hbm, ...), custom_call_target="tpu_custom_call" | custom-call | tf_op jit(solution)/shard_map/gradient_sums/pallas_call | solution.py:1406
  193.4 24.2 %final_update.1 = (f32[1,1]{1,0:T(1,128)}, f32[128,256]{1,0:T(8,128)}, f32[128,256]{1,0:T(8,128)}, f32[128,256]{1,0:T(8,128)}, bf16[128,256]{1,0:T(8,128)(2,1)},...) custom-call(bf16[1024,128]{1,0:T(8,128)(2,1)} %get-tuple-element.77., ...), custom_call_target="tpu_custom_call" | custom-call | tf_op jit(solution)/shard_map/final_update/pallas_call | solution.py:1541
